TPU v7x, 512 devices: a whole 4x4x16 slice. The times are simulated.
512 devices in a mesh: fsdp: 32 (over z, core), tp: 16 (over x, y).
Axes of the slice: x: 4, y: 4, z: 16, core: 2. Of those that a mesh axis runs over, the one named last changes fastest.
Arguments:
- gradient: bfloat16 [8192, 28672], P('fsdp', 'tp'), may hold values from -6 to 6
- momentum: bfloat16 [8192, 28672], P('fsdp', 'tp'), may hold values from -6 to 6
- right_factor: bfloat16 [28672, 256], P(('tp', 'fsdp')), may hold values from -0.03125 to 0.03125
Outputs:
- update: bfloat16 [8192, 28672], P('fsdp', 'tp')
- new_momentum: bfloat16 [8192, 28672], P('fsdp', 'tp')
- new_right: bfloat16 [28672, 256], P(('tp', 'fsdp'))
All inputs are finite; a program needn't handle non-finite values.
Results may differ from a plain program's by a relative error of at most 0.0085.
Values may be sent and summed in bfloat16 or wider, within the bound.
A program may use at most 64 MiB of HBM per device.

v0:
```python
import math

import jax
import jax.numpy as jnp
from jax import lax
from jax.sharding import PartitionSpec as P

D = 8192
FF = 28672
RANK = 256


epsilon = 1e-06
feedback = 0.1


def orthonormal(basis, gram_matrix):
    lower = jnp.linalg.cholesky(gram_matrix)
    return jax.scipy.linalg.solve_triangular(lower, basis.T, lower=True).T.astype(jnp.bfloat16)


def shards(gradient, momentum, right_factor):
    blend = momentum.astype(jnp.float32) + gradient.astype(jnp.float32)
    blend_b = blend.astype(jnp.bfloat16)
    row_count = right_factor.shape[0]
    partial_basis = jnp.dot(
        blend_b,
        lax.all_gather(right_factor, "fsdp", axis=0, tiled=True),
        preferred_element_type=jnp.float32,
    )
    basis = lax.psum(partial_basis, "tp")
    gram_local = jnp.dot(basis.T, basis, precision=lax.Precision.HIGHEST)
    gram_matrix = lax.psum(gram_local, "fsdp")
    ortho_b = orthonormal(basis, gram_matrix)
    contract_rows = (((0,), (0,)), ((), ()))
    partial_proj = lax.dot_general(
        blend_b, ortho_b, contract_rows, preferred_element_type=jnp.float32
    )
    projected = lax.psum(partial_proj, "fsdp")
    col_sums = lax.psum(jnp.sum(projected * projected, axis=0), "tp")
    right_block = (projected * lax.rsqrt(col_sums + epsilon)).astype(jnp.bfloat16)
    projected_b = projected.astype(jnp.bfloat16)
    new_right = lax.dynamic_slice_in_dim(
        right_block, lax.axis_index("fsdp") * row_count, row_count, 0
    )
    contract_cols = (((1,), (1,)), ((), ()))
    rank_term = lax.dot_general(
        ortho_b, projected_b, contract_cols, preferred_element_type=jnp.float32
    )
    new_momentum = (blend - feedback * rank_term).astype(jnp.bfloat16)
    rms_scale = math.sqrt(D * FF / RANK)
    direction = lax.dot_general(
        ortho_b, right_block, contract_cols, preferred_element_type=jnp.float32
    )
    update = (rms_scale * direction).astype(jnp.bfloat16)
    return (update, new_momentum, new_right)


def solution(mesh):
    in_specs = (P("fsdp", "tp"), P("fsdp", "tp"), P(("tp", "fsdp"), None))
    out_specs = (P("fsdp", "tp"), P("fsdp", "tp"), P(("tp", "fsdp"), None))
    return jax.shard_map(shards, mesh=mesh, in_specs=in_specs, out_specs=out_specs, check_vma=False)
```

profile of v0, /device:TPU:1, one launch (start us, length us, event | category | flops | bytes accessed | tf_op | source)
XLA Modules:
  0.0 692.6 jit_solution(4357019867133229550)
XLA Ops:
  7.2 0.0 all-reduce.5.cloned.1.call-start
  7.2 40.3 %all_gather.3 = bf16[1792,256]{1,0:T(8,128)(2,1)S(1)} all-gather(bf16[56,256]{1,0:T(8,128)(2,1)} %param.5), channel_id=1, replica_groups=mesh['fsdp'=32,'tp'=16] {'fsdp'}, dimensions={0}, use_global_device_ids=true | all-gather | bytes 946176 | tf_op jit(solution)/shard_map/all_gather | solution.py:28
  47.5 2.6 fusion.7
  50.1 0.0 all-reduce.5.cloned.1.call-update
  50.1 0.0 all-reduce.7.cloned.1.call-start
  50.2 109.3 %all-reduce.5.cloned.1.call-done = f32[256,256]{1,0:T(8,128)} async-done(((f32[256,256]{1,0:T(8,128)}), f32[256,256]{1,0:T(8,128)}) %all-reduce.5.cloned.1.call-update) | async-done | bytes 262160 | tf_op jit(solution)/shard_map/psum | solution.py:31
  159.5 2.3 fusion.21
  161.8 0.0 all-reduce.7.cloned.1.call-update
  161.8 0.0 all-reduce.9.cloned.1.call-start
  161.9 207.6 %all-reduce.7.cloned.1.call-done = f32[256,256]{0,1:T(8,128)} async-done(((f32[256,256]{0,1:T(8,128)}), f32[256,256]{0,1:T(8,128)}) %all-reduce.7.cloned.1.call-update) | async-done | bytes 262160 | tf_op jit(solution)/shard_map/psum | solution.py:33
  369.5 1.1 copy.7
  370.6 0.0 copy-start.4
  370.6 1.0 fusion.9
  371.6 0.0 copy-start.1
  371.6 0.0 copy-start.2
  371.6 11.7 %cholesky.50 = f32[128,128]{1,0:T(8,128)S(1)} custom-call(f32[128,128]{1,0:T(8,128)S(1)} %cholesky.118), custom_call_target="Cholesky" | custom-call | tf_op jit(solution)/shard_map/jit(cholesky)/cholesky | solution.py:18
  383.4 9.8 %custom-call.15 = f32[1,128,128]{1,2,0:T(8,128)S(1)} custom-call(f32[1,128,128]{2,1,0:T(8,128)S(1)} %get-tuple-element.24), custom_call_target="InvertDiagBlocksLowerTriangular" | custom-call | tf_op jit(solution)/shard_map/jit(cholesky)/cholesky | solution.py:18
  393.2 0.2 constant_dynamic-update-slice_fusion
  393.4 0.3 convolution_subtract_fusion.1
  393.7 11.7 %cholesky.105 = f32[128,128]{1,0:T(8,128)S(1)} custom-call(f32[128,128]{1,0:T(8,128)S(1)} %convolution_subtract_fusion.1), custom_call_target="Cholesky" | custom-call | tf_op jit(solution)/shard_map/jit(cholesky)/cholesky | solution.py:18
  405.5 0.6 compare_reduce_fusion
  407.4 0.1 triangular_solve.57
  407.5 4.1 while.1
  407.7 0.6 fusion.31
  408.2 1.4 bitcast_dynamic-update-slice_fusion.2
  409.7 0.6 fusion.31
  410.2 1.4 bitcast_dynamic-update-slice_fusion.2
  411.6 19.7 %custom-call.16 = f32[2,128,128]{1,2,0:T(8,128)S(1)} custom-call(f32[2,128,128]{2,1,0:T(8,128)S(1)} %get-tuple-element.10), custom_call_target="InvertDiagBlocksLowerTriangular" | custom-call | tf_op jit(solution)/shard_map/jit(_solve_triangular)/triangular_solve | solution.py:19
  431.3 0.0 copy-done.4
  431.3 0.3 fusion.20
  431.7 0.4 convolution_subtract_fusion
  432.1 0.3 convolution_convert_fusion
  432.4 0.0 copy-done.1
  432.4 0.0 copy-done.2
  432.4 1.7 fusion.5
  434.1 0.0 all-reduce.9.cloned.1.call-update
  434.1 213.1 %all-reduce.9.cloned.1.call-done = f32[1792,256]{1,0:T(8,128)} async-done(((f32[1792,256]{1,0:T(8,128)}), f32[1792,256]{1,0:T(8,128)}) %all-reduce.9.cloned.1.call-update) | async-done | bytes 1835024 | tf_op jit(solution)/shard_map/psum | solution.py:39
  647.2 0.0 copy-start
  647.2 1.9 multiply_reduce_fusion
  649.1 33.3 %psum.31 = f32[256]{0:T(256)S(1)} all-reduce(f32[256]{0:T(256)S(1)} %multiply_reduce_fusion), channel_id=1, replica_groups=mesh['fsdp'=32,'tp'=16] {'tp'}, use_global_device_ids=true, to_apply=%region_8.9 | all-reduce | flops 256 | bytes 2048 | tf_op jit(solution)/shard_map/psum | solution.py:40
  682.4 0.0 copy-done
  682.4 0.0 copy-start.3
  682.4 0.1 multiply_convert_fusion
  682.6 1.4 fusion.1
  684.0 0.6 constant_dynamic-slice_fusion.1
  684.6 0.0 copy-done.3
  684.6 1.5 fusion.2
  (10 shorter events, 0.2 us)
Async XLA Ops:
  7.2 152.3 %all-reduce.5.cloned.1.call-start = ((), (), s32[]{:S(2)}) async-start(), calls=%async_computation | async-start | bytes 524288 | tf_op jit(solution)/shard_map/psum | solution.py:31
  50.1 319.3 %all-reduce.7.cloned.1.call-start = ((), (), s32[]{:S(2)}) async-start(), calls=%async_computation.1 | async-start | bytes 524288 | tf_op jit(solution)/shard_map/psum | solution.py:33
  161.8 485.4 %all-reduce.9.cloned.1.call-start = ((), (), s32[]{:S(2)}) async-start(), calls=%async_computation.2 | async-start | bytes 3670016 | tf_op jit(solution)/shard_map/psum | solution.py:39
  370.6 60.8 %copy-start.4 = (f32[256,256]{1,0:T(8,128)S(1)}, f32[256,256]{1,0:T(8,128)}, u32[]{:S(2)}) copy-start(f32[256,256]{1,0:T(8,128)} %all-reduce.5.cloned.1.call-done) | copy-start | bytes 786436
  371.6 60.8 %copy-start.1 = (bf16[256,1792]{1,0:T(8,128)(2,1)S(1)}, bf16[256,1792]{1,0:T(8,128)(2,1)}, u32[]{:S(2)}) copy-start(bf16[256,1792]{1,0:T(8,128)(2,1)} %param.3) | copy-start | bytes 2752516
  371.6 60.8 %copy-start.2 = (bf16[256,1792]{1,0:T(8,128)(2,1)S(1)}, bf16[256,1792]{1,0:T(8,128)(2,1)}, u32[]{:S(2)}) copy-start(bf16[256,1792]{1,0:T(8,128)(2,1)} %param.4) | copy-start | bytes 2752516
  647.2 35.2 %copy-start = (f32[1792,256]{1,0:T(8,128)S(1)}, f32[1792,256]{1,0:T(8,128)}, u32[]{:S(2)}) copy-start(f32[1792,256]{1,0:T(8,128)} %all-reduce.9.cloned.1.call-done) | copy-start | bytes 5505028
  682.4 2.2 copy-start.3
Sparse Core Ops, SparseCore 0:
  50.3 109.1 all-reduce.4
  162.5 206.9 all-reduce.6
  434.2 212.9 all-reduce.8
where the time goes:
time: 696 us; the launch traced here: 693 us
  waiting for transfers between devices  530 us (76%)
  blocking collectives  73.7 us (11%)
  other arithmetic  56.7 us (8%)
  between operations  15.2 us (2%)
  matrix products  10.9 us (2%)
    psum x1, waiting for transfers between devices, shards(): projected = lax.psum(partial_proj, 'fsdp')  213 us
    psum x1, waiting for transfers between devices, shards(): gram_matrix = lax.psum(gram_local, 'fsdp')  208 us
    psum x1, waiting for transfers between devices, shards(): basis = lax.psum(partial_basis, 'tp')  109 us
    all_gather x1, blocking collectives, shards(): lax.all_gather(right_factor, 'fsdp', axis=0, tiled=True)  40.3 us
    another operation x6, other arithmetic, orthonormal(): lower = jnp.linalg.cholesky(gram_matrix)  34 us
    psum x1, blocking collectives, shards(): col_sums = lax.psum(jnp.sum(projected * projected, axis=0), 'tp')  33.3 us
    another operation x3, other arithmetic, orthonormal(): jax.scipy.linalg.solve_triangular(lower, basis.T, lower=True)  19.7 us
  transfers between devices with their start and end apart: 3, of which 3 were waited for; matrix products, arithmetic and copies ran while one was open for 0% of the time, Pallas kernels for 0%

commit v1 on v0

v1 whole, which is shorter than its diff:
```python
import functools
import math

import jax
import jax.numpy as jnp
from jax import lax
from jax.experimental import pallas as pl
from jax.experimental.pallas import tpu as pltpu
from jax.sharding import PartitionSpec as P

D = 8192
FF = 28672
RANK = 256

epsilon = 1e-06
feedback = 0.1

F32 = jnp.float32
BF16 = jnp.bfloat16
MESH = pl.DeviceIdType.MESH
HIGHEST = lax.Precision.HIGHEST
LANES = 128
PIVOTS = 32
NEAR = (1, -1, 2, -2)
FAR = (5, -5)
RELAY_AT = 64
VMEM_LIMIT = 62 * 1024 * 1024


class Place:
    def __init__(self, chips, tensors):
        self.chips, self.tensors = chips, tensors
        self.f = lax.axis_index("fsdp")
        self.t = lax.axis_index("tp")
        self.z = lax.div(self.f, 2)
        self.c = lax.rem(self.f, 2)

    def chip(self, steps):
        return lax.rem(self.z + steps + self.chips, self.chips)

    def on_chip(self, z):
        return (z * 2 + self.c, self.t)

    def partner(self):
        return (self.z * 2 + 1 - self.c, self.t)

    def tensor(self, steps):
        return lax.rem(self.t + steps, self.tensors)


def remote(src, dst, send_sem, recv_sem, device):
    return pltpu.make_async_remote_copy(
        src_ref=src,
        dst_ref=dst,
        send_sem=send_sem,
        recv_sem=recv_sem,
        device_id=device,
        device_id_type=MESH,
    )


class Exchange:
    def __init__(self, place, chips, src, dst, arrived, send_sem, recv_sem, unroll):
        self.all = remote(arrived, arrived, send_sem, recv_sem, place.partner())

        def start(i, _):
            if chips:
                peer = place.chip(i)
                device = place.on_chip(peer)
            else:
                peer = place.tensor(i)
                device = (place.f, peer)
            remote(src(peer), dst, send_sem, recv_sem, device).start()
            return 0

        count = place.chips if chips else place.tensors
        if unroll:
            for i in range(1, count):
                start(i, 0)
        else:
            lax.fori_loop(1, count, start, 0)

    def wait_recv(self):
        self.all.wait_recv()

    def wait_send(self):
        self.all.wait_send()


class Gather:
    def __init__(self, place, slots, sems, recv_sem):
        self.place, self.slots = place, slots
        self.send_sem, self.send_part, self.recv_part = (sems.at[i] for i in range(3))
        self.recv_sem = recv_sem
        self.relayed = []

    def slot(self, chip):
        return self.slots.at[chip, self.place.c]

    def send(self, kind, chip, steps):
        ref = self.slot(chip)
        device = self.place.on_chip(self.place.chip(steps))
        remote(ref, ref, self.send_sem, self.recv_sem.at[kind], device).start()

    def arrived(self, kind, chip):
        ref = self.slot(chip)
        remote(ref, ref, self.send_sem, self.recv_sem.at[kind], self.place.partner()).wait_recv()

    def forward(self, chip):
        ref = self.slot(chip)
        remote(ref, ref, self.send_part, self.recv_part, self.place.partner()).start()

    def begin(self):
        for kind, steps in enumerate(FAR + NEAR):
            self.send(kind, self.place.z, steps)
        self.forward(self.place.z)

    def relay(self):
        place = self.place
        for i, far in enumerate(FAR):
            chip = place.chip(-far)
            self.arrived(i, chip)
            for j, near in enumerate(NEAR):
                self.send(6 + 4 * i + j, chip, near)
            self.forward(chip)
        self.send(14, place.chip(5 - 10 * place.c), 6 * place.c - 3)

    def finish(self):
        place = self.place
        for i, near in enumerate(NEAR):
            chip = place.chip(-near)
            self.arrived(2 + i, chip)
            self.forward(chip)
        for i, far in enumerate(FAR):
            for j, near in enumerate(NEAR):
                chip = place.chip(-far - near)
                self.arrived(6 + 4 * i + j, chip)
                self.forward(chip)
        self.arrived(14, place.chip(8))
        self.forward(place.chip(8))
        self.half().wait_recv()

    def half(self):
        ref = self.slots.at[:, 0]
        return remote(ref, ref, self.send_part, self.recv_part, self.place.partner())

    def drain(self):
        self.half().wait_send()
        ref = self.slots.at[: self.place.chips - 1, 0]
        remote(ref, ref, self.send_sem, self.recv_part, self.place.partner()).wait_send()


class Sum:
    def __init__(self, place, prepare, terms, relays, direct, sums, send_sem, recv_sem):
        self.place, self.terms = place, terms
        self.prepare = prepare
        self.relays, self.direct, self.sums = relays, direct, sums
        self.send_sem, self.recv_sem = send_sem, recv_sem
        self.started = {}

    def send(self, kind, src, into, steps):
        device = self.place.on_chip(self.place.chip(steps))
        copy = remote(src, into, self.send_sem, self.recv_sem.at[kind], device)
        copy.start()
        self.started[kind] = copy

    def begin(self):
        place = self.place
        for i, far in enumerate(FAR):
            for j, near in enumerate(NEAR):
                self.prepare(place.chip(near + far))
                self.send(4 * i + j, self.terms.at[place.chip(near + far)], self.relays.at[4 * i + j], near)
        self.prepare(place.chip(8))
        self.send(14, self.terms.at[place.chip(8)], self.relays.at[8], 3 - 6 * place.c)
        for j, near in enumerate(NEAR):
            self.prepare(place.chip(near))
            self.send(8 + j, self.terms.at[place.chip(near)], self.direct.at[j], near)
        for far in FAR:
            self.prepare(place.chip(far))
        self.prepare(place.z)

    def relay(self):
        for i, far in enumerate(FAR):
            value = self.terms[self.place.chip(far)]
            for j in range(4):
                self.started[4 * i + j].wait_recv()
                value = value + self.relays[4 * i + j]
            if i == 0:
                self.started[14].wait_recv()
            self.sums[i] = value + jnp.where(self.place.c == i, self.relays[8], 0.0)
            self.send(12 + i, self.sums.at[i], self.direct.at[4 + i], far)

    def finish(self):
        value = self.terms[self.place.z]
        for kind in range(8, 14):
            self.started[kind].wait_recv()
            value = value + self.direct[kind - 8]
        return value

    def drain(self):
        ref = self.terms.at[: self.place.chips - 1]
        remote(ref, ref, self.send_sem, self.recv_sem.at[0], self.place.partner()).wait_send()


def total(ref, count):
    value = ref[0]
    for i in range(1, count):
        value = value + ref[i]
    return value


def packed(value):
    return jnp.concatenate([value[:, :LANES], value[:, LANES:]], axis=0).astype(BF16)


def unpack(slots, chips, block, out, ready=None):
    quarter = chips // 4
    for k in range(chips):
        pair = [slots[k, core].astype(F32) for core in range(2)]
        for half in range(2):
            rows = jnp.concatenate([value[half * block : (half + 1) * block] for value in pair], axis=0)
            out[2 * block * k : 2 * block * (k + 1), half * LANES : (half + 1) * LANES] = rows.astype(BF16)
        if ready and (k + 1) % quarter == 0:
            ready(slice(2 * block * (k + 1 - quarter), 2 * block * (k + 1)))


def eliminate(left, right, scale, first):
    n = left.shape[0]
    tiles = n // LANES
    groups = PIVOTS // 8
    in_group = lax.broadcasted_iota(jnp.int32, (8, LANES), 0)
    tile0 = first // LANES
    left_tiles = list(range(tile0, tiles))
    right_tiles = list(range(0, tile0 + 1))

    def load(ref, g, tile):
        return ref[first + 8 * g : first + 8 * g + 8, tile * LANES : (tile + 1) * LANES]

    s = {tile: [load(left, g, tile) for g in range(groups)] for tile in left_tiles}
    m = {tile: [load(right, g, tile) for g in range(groups)] for tile in right_tiles}
    inverse = [jnp.zeros((8, LANES), F32) for _ in range(groups)]
    for sub in range(groups):
        lane = first + 8 * sub - tile0 * LANES
        column = [
            {
                g: jnp.broadcast_to(s[tile0][g][:, lane + j : lane + j + 1], (8, LANES))
                for g in range(sub, groups)
            }
            for j in range(8)
        ]
        for j in range(0, 8, 2):
            col0, col1 = column[j], column[j + 1]
            a = col0[sub][j : j + 1, :]
            b = col1[sub][j : j + 1, :]
            c = col1[sub][j + 1 : j + 2, :]
            recip0 = 1.0 / a
            recip1 = a * (1.0 / (a * c - b * b))
            lower = b * recip0
            inverse[sub] = jnp.where(in_group == j, recip0, jnp.where(in_group == j + 1, recip1, inverse[sub]))
            factors = {}
            for g in range(sub, groups):
                factor0 = col0[g] * recip0
                factor1 = (col1[g] - col0[g] * lower) * recip1
                if g == sub:
                    factor0 = jnp.where(in_group > j, factor0, 0.0)
                    factor1 = jnp.where(in_group > j + 1, factor1, 0.0)
                factors[g] = (factor0, factor1)

            def reduce(parts):
                row0 = parts[sub][j : j + 1, :]
                row1 = parts[sub][j + 1 : j + 2, :] - lower * row0
                for g, (factor0, factor1) in factors.items():
                    parts[g] = (parts[g] - factor0 * row0) - factor1 * row1

            for k in range(j + 2, 8):
                reduce(column[k])
            for tile in left_tiles:
                reduce(s[tile])
            for tile in right_tiles:
                reduce(m[tile])
    for g in range(groups):
        rows = slice(first + 8 * g, first + 8 * g + 8)
        scale[rows, :] = inverse[g]
        for tile in right_tiles:
            right[rows, tile * LANES : (tile + 1) * LANES] = m[tile][g]
    done = first + PIVOTS
    if done == n:
        return

    def joined(parts):
        return jnp.concatenate(parts, axis=0)

    lower0 = tile0 * LANES
    s_rows = {tile: joined(s[tile]) for tile in left_tiles}
    m_rows = {tile: joined(m[tile]) for tile in right_tiles}
    scaled = jnp.concatenate([s_rows[tile] * joined(inverse) for tile in left_tiles], axis=1)
    both = jnp.concatenate([s_rows[tile] for tile in left_tiles] + [m_rows[tile] for tile in right_tiles], axis=1)
    change = lax.dot_general(
        scaled, both, (((0,), (0,)), ((), ())), precision=HIGHEST, preferred_element_type=F32
    )
    below = slice(done - lower0, n - lower0)
    wide = len(left_tiles) * LANES
    left[done:, lower0:] = left[done:, lower0:] - change[below, :wide]
    right[done:, : len(right_tiles) * LANES] = right[done:, : len(right_tiles) * LANES] - change[below, wide:]


def main_kernel(
    chips, tensors,
    g_ref, m_ref, r_ref, ortho_out, projected_out, own_out, norm_out,
    g_here, m_here, r_here, blend_b, slots, right_all, partial, parts, basis, gram, other, pieces, gathered,
    left, right, scale, product, from_partner, terms, relays, direct, relay_sums, projected_slots,
    squares, other_squares, square_parts, square_rows, ortho, projected, own_rows, norm,
    load_sem, sems_r, recv_r, send_q, recv_q, send_h, recv_h, sems_p, recv_p, send_t, recv_t, send_z, recv_z, send_o, recv_o, store_sem,
):
    place = Place(chips, tensors)
    rows, width = g_ref.shape
    block, rank = r_ref.shape
    share = rows // tensors
    piece = rank // tensors // 2
    tile = math.gcd(width, 256)
    drains = []
    barrier = pltpu.get_barrier_semaphore()

    def greet(device):
        pl.semaphore_signal(barrier, inc=1, device_id=device, device_id_type=MESH)

    def greet_chip(i, _):
        greet(place.on_chip(place.chip(i)))
        return 0

    def greet_tensor(i, _):
        greet((place.f, place.tensor(i)))
        return 0

    loads = [
        pltpu.make_async_copy(src, dst, load_sem.at[i])
        for i, (src, dst) in enumerate(((r_ref, r_here), (g_ref, g_here), (m_ref, m_here)))
    ]
    loads[0].start()
    greet(place.partner())
    lax.fori_loop(1, chips, greet_chip, 0)
    lax.fori_loop(1, tensors, greet_tensor, 0)
    for load in loads[1:]:
        load.start()
    loads[0].wait()
    slots[place.z, place.c] = packed(r_here[...].astype(F32))
    pl.semaphore_wait(barrier, tensors + chips - 1)

    stores = []

    def store(src, dst):
        copy = pltpu.make_async_copy(src, dst, store_sem.at[len(stores)])
        copy.start()
        stores.append(copy)

    def exchange(chips, index, src, dst, arrived, unroll=True):
        sems = (send_z, recv_z) if chips else (send_t, recv_t)
        new = Exchange(place, chips, src, dst, arrived, sems[0].at[index], sems[1].at[index], unroll)
        drains.append(new.wait_send)
        return new

    def swap(index, src, dst):
        new = remote(src, dst, send_o.at[index], recv_o.at[index], place.partner())
        new.start()
        drains.append(new.wait_send)
        return new

    with jax.named_scope("gather_right"):
        gather = Gather(place, slots, sems_r, recv_r)
        gather.begin()
        drains.append(gather.drain)
        for load in loads[1:]:
            load.wait()
        for j in range(0, width, tile):
            columns = slice(j, j + tile)
            blend_b[:, columns] = (m_here[:, columns].astype(F32) + g_here[:, columns].astype(F32)).astype(BF16)
        gather.relay()
        gather.finish()
    unpack(slots, chips, block, right_all)
    partial[...] = jnp.dot(blend_b[...], right_all[...], preferred_element_type=F32)

    def share_of(ref, t):
        return ref.at[pl.ds(pl.multiple_of(t * share, share), share), :]

    with jax.named_scope("sum_basis"):
        work = exchange(False, 0, lambda t: share_of(partial, t), parts.at[place.t], parts.at[: tensors - 1])
        parts[place.t] = share_of(partial, place.t)[...]
        work.wait_recv()
        mine = share_of(basis, place.t)
        mine[...] = total(parts, tensors)
        exchange(False, 1, lambda t: mine, mine, basis.at[: rows - share]).wait_recv()

    contract_rows = (((0,), (0,)), ((), ()))
    contract_columns = (((1,), (1,)), ((), ()))
    value = basis[...]
    gram[...] = lax.dot_general(value, value, contract_rows, precision=HIGHEST, preferred_element_type=F32)

    def piece_of(core):
        return gram.at[pl.ds(pl.multiple_of((place.t * 2 + core) * piece, piece), piece), :]

    gram_swap = swap(0, piece_of(1 - place.c), other)

    splits = []
    for _ in range(3):
        splits.append(value.astype(BF16))
        value = value - splits[-1].astype(F32)
    basis_b = jnp.concatenate(splits, axis=1)
    for j in range(0, width, tile):
        part = lax.dot_general(blend_b[:, j : j + tile], basis_b, contract_rows, preferred_element_type=F32)
        part = part[:, :rank] + part[:, rank : 2 * rank] + part[:, 2 * rank :]
        at = j
        while at < j + tile:
            chunk, skip = divmod(at, block)
            most = min(block - skip, j + tile - at)
            product[chunk // 2, chunk % 2, skip : skip + most, :] = part[at - j : at - j + most]
            at += most
    order = [place.chip(near + far) for far in FAR for near in NEAR] + [place.chip(8)]
    order += [place.chip(steps) for steps in NEAR + FAR] + [place.z]
    halves = []
    for i, chip in enumerate(order):
        half = remote(
            product.at[chip, 1 - place.c], from_partner.at[chip], send_h.at[0], recv_h.at[i], place.partner()
        )
        half.start()
        halves.append(half)

    gram_swap.wait_recv()
    pieces[place.z] = piece_of(place.c)[...] + other[...]
    with jax.named_scope("sum_gram"):
        gram_work = exchange(
            True, 0, lambda z: pieces.at[place.z], pieces.at[place.z], pieces.at[: chips - 1]
        )
        waiting = list(halves)

        def add_cores(chip):
            waiting.pop(0).wait_recv()
            terms[chip] = product[chip, place.c] + from_partner[chip]

        chip_sum = Sum(place, add_cores, terms, relays, direct, relay_sums, send_q.at[0], recv_q)
        chip_sum.begin()
        for drain in drains:
            drain()
        drains.clear()
        drains.append(chip_sum.drain)
        drains.append(
            remote(from_partner, from_partner, send_h.at[0], recv_h.at[0], place.partner()).wait_send
        )
        gram_work.wait_recv()
        gathered[place.c, place.t] = total(pieces, chips)
        own = gathered.at[place.c, place.t]
        exchange(False, 2, lambda t: own, own, gathered.at[0, : tensors - 1]).wait_recv()
        swap(1, gathered.at[place.c], gathered.at[place.c]).wait_recv()
    for t in range(tensors):
        for core in range(2):
            at = (t * 2 + core) * piece
            left[at : at + piece, :] = gathered[core, t]

    at_row = lax.broadcasted_iota(jnp.int32, (rank, rank), 0)
    at_column = lax.broadcasted_iota(jnp.int32, (rank, rank), 1)
    right[...] = jnp.where(at_row == at_column, 1.0, 0.0).astype(F32)
    value = left[...]
    diagonal = jnp.where(at_row == at_column, value, 0.0)
    to_unit = lax.rsqrt(jnp.sum(diagonal, axis=0, keepdims=True))
    left[...] = value * lax.rsqrt(jnp.sum(diagonal, axis=1, keepdims=True)) * to_unit
    with jax.named_scope("factor"):
        for first in range(0, rank, PIVOTS):
            if first == RELAY_AT:
                chip_sum.relay()
            eliminate(left, right, scale, first)
    inverse_lower = jnp.concatenate(
        [right[:, at : at + LANES] * jnp.sqrt(scale[...]) for at in range(0, rank, LANES)], axis=1
    ) * to_unit
    value = lax.dot_general(
        chip_sum.finish(), inverse_lower, contract_columns, precision=HIGHEST, preferred_element_type=F32
    )
    projected_slots[place.z, place.c] = packed(value)
    with jax.named_scope("gather_projected"):
        gather = Gather(place, projected_slots, sems_p, recv_p)
        gather.begin()
        drains.append(gather.drain)
        squares[...] = jnp.sum((value * value).reshape(block // 8, 8, rank), axis=0)
        square_swap = swap(3, squares, other_squares)
        own_rows[...] = value
        store(own_rows, own_out)
        ortho[...] = lax.dot_general(
            basis[...], inverse_lower, contract_columns, precision=HIGHEST, preferred_element_type=F32
        ).astype(BF16)
        store(ortho, ortho_out)
        square_swap.wait_recv()
        square_parts[place.t] = squares[...] + other_squares[...]
        mine = square_parts.at[place.t]
        work = exchange(False, 3, lambda t: mine, mine, square_parts.at[: tensors - 1], False)
        gather.relay()
        work.wait_recv()
        square_rows[place.z] = jnp.sum(total(square_parts, tensors), axis=0, keepdims=True)
        mine_row = square_rows.at[place.z]
        work = exchange(True, 1, lambda z: mine_row, mine_row, square_rows.at[: chips - 1], False)
        gather.finish()
        work.wait_recv()
    norm[...] = jnp.broadcast_to(lax.rsqrt(total(square_rows, chips) + epsilon), norm.shape)
    store(norm, norm_out)
    unpack(
        projected_slots, chips, block, projected,
        lambda rows: store(projected.at[rows, :], projected_out.at[rows, :]),
    )
    for drain in drains:
        drain()
    for copy in stores:
        copy.wait()


def output_kernel(
    g_ref, m_ref, o_ref, p_ref, own_ref, norm_ref, update_out, momentum_out, right_out,
    g_here, m_here, p_here, update, momentum, o_here, own_here, norm_here, right_here,
    load_sem, store_sem, small_sem,
):
    width = g_ref.shape[1]
    step = math.gcd(width, 256)
    spans = [slice(at, min(at + 2 * step, width)) for at in range(0, width, 2 * step)]
    small = [
        pltpu.make_async_copy(src, dst, small_sem.at[i])
        for i, (src, dst) in enumerate(((o_ref, o_here), (norm_ref, norm_here), (own_ref, own_here)))
    ]
    for copy in small:
        copy.start()
    loads = []
    for i, span in enumerate(spans):
        copies = [
            pltpu.make_async_copy(p_ref.at[span, :], p_here.at[span, :], load_sem.at[0, i]),
            pltpu.make_async_copy(g_ref.at[:, span], g_here.at[:, span], load_sem.at[1, i]),
            pltpu.make_async_copy(m_ref.at[:, span], m_here.at[:, span], load_sem.at[2, i]),
        ]
        for copy in copies:
            copy.start()
        loads.append(copies)
    contract = (((1,), (1,)), ((), ()))
    for copy in small:
        copy.wait()
    ortho_b = o_here[...]
    norm = norm_here[0:1, :]
    right_here[...] = (own_here[...] * norm).astype(BF16)
    stores = [pltpu.make_async_copy(right_here, right_out, small_sem.at[3])]
    stores[0].start()
    for i, span in enumerate(spans):
        for copy in loads[i]:
            copy.wait()
        for at in range(span.start, span.stop, step):
            columns = slice(at, at + step)
            projected = p_here[columns, :]
            term = lax.dot_general(ortho_b, projected, contract, preferred_element_type=F32)
            blend = m_here[:, columns].astype(F32) + g_here[:, columns].astype(F32)
            momentum[:, columns] = (blend - feedback * term).astype(BF16)
            new_right = (projected.astype(F32) * norm).astype(BF16)
            term = lax.dot_general(ortho_b, new_right, contract, preferred_element_type=F32)
            update[:, columns] = (math.sqrt(D * FF / RANK) * term).astype(BF16)
        copies = [
            pltpu.make_async_copy(momentum.at[:, span], momentum_out.at[:, span], store_sem.at[0, i]),
            pltpu.make_async_copy(update.at[:, span], update_out.at[:, span], store_sem.at[1, i]),
        ]
        for copy in copies:
            copy.start()
        stores += copies
    for copy in stores:
        copy.wait()


def shards(chips, tensors, gradient, momentum, right_factor):
    rows, width = gradient.shape
    block, rank = right_factor.shape
    piece = rank // tensors // 2
    anywhere = pl.BlockSpec(memory_space=pl.ANY)

    def dma(*shape):
        return pltpu.SemaphoreType.DMA(shape)

    ortho_b, projected, own, norm = pl.pallas_call(
        functools.partial(main_kernel, chips, tensors),
        out_shape=[
            jax.ShapeDtypeStruct((rows, rank), BF16),
            jax.ShapeDtypeStruct((width, rank), BF16),
            jax.ShapeDtypeStruct((block, rank), F32),
            jax.ShapeDtypeStruct((8, rank), F32),
        ],
        in_specs=[anywhere] * 3,
        out_specs=[anywhere] * 4,
        scratch_shapes=[
            pltpu.VMEM((rows, width), BF16),
            pltpu.VMEM((rows, width), BF16),
            pltpu.VMEM((block, rank), BF16),
            pltpu.VMEM((rows, width), BF16),
            pltpu.VMEM((chips, 2, 2 * block, LANES), BF16),
            pltpu.VMEM((width, rank), BF16),
            pltpu.VMEM((rows, rank), F32),
            pltpu.VMEM((tensors, rows // tensors, rank), F32),
            pltpu.VMEM((rows, rank), F32),
            pltpu.VMEM((rank, rank), F32),
            pltpu.VMEM((piece, rank), F32),
            pltpu.VMEM((chips, piece, rank), F32),
            pltpu.VMEM((2, tensors, piece, rank), F32),
            pltpu.VMEM((rank, rank), F32),
            pltpu.VMEM((rank, rank), F32),
            pltpu.VMEM((rank, LANES), F32),
            pltpu.VMEM((chips, 2, block, rank), F32),
            pltpu.VMEM((chips, block, rank), F32),
            pltpu.VMEM((chips, block, rank), F32),
            pltpu.VMEM((9, block, rank), F32),
            pltpu.VMEM((6, block, rank), F32),
            pltpu.VMEM((2, block, rank), F32),
            pltpu.VMEM((chips, 2, 2 * block, LANES), BF16),
            pltpu.VMEM((8, rank), F32),
            pltpu.VMEM((8, rank), F32),
            pltpu.VMEM((tensors, 8, rank), F32),
            pltpu.VMEM((chips, 1, rank), F32),
            pltpu.VMEM((rows, rank), BF16),
            pltpu.VMEM((width, rank), BF16),
            pltpu.VMEM((block, rank), F32),
            pltpu.VMEM((8, rank), F32),
            dma(3), dma(3), dma(chips - 1), dma(1), dma(chips - 1), dma(1), dma(chips), dma(3), dma(chips - 1),
            dma(4), dma(4), dma(2), dma(2), dma(4), dma(4), dma(7),
        ],
        compiler_params=pltpu.CompilerParams(
            collective_id=0, has_side_effects=True, vmem_limit_bytes=VMEM_LIMIT
        ),
        name="main",
    )(gradient, momentum, right_factor)

    spans = -(-width // (2 * math.gcd(width, 256)))
    whole = pltpu.VMEM((rows, width), BF16)
    return pl.pallas_call(
        output_kernel,
        out_shape=[
            jax.ShapeDtypeStruct((rows, width), BF16),
            jax.ShapeDtypeStruct((rows, width), BF16),
            jax.ShapeDtypeStruct((block, rank), BF16),
        ],
        in_specs=[anywhere] * 6,
        out_specs=[anywhere] * 3,
        scratch_shapes=[
            whole, whole, pltpu.VMEM((width, rank), BF16), whole, whole,
            pltpu.VMEM((rows, rank), BF16), pltpu.VMEM((block, rank), F32), pltpu.VMEM((8, rank), F32),
            pltpu.VMEM((block, rank), BF16),
            dma(3, spans), dma(2, spans), dma(4),
        ],
        compiler_params=pltpu.CompilerParams(vmem_limit_bytes=VMEM_LIMIT),
        name="output",
    )(gradient, momentum, ortho_b, projected, own, norm)


def solution(mesh):
    chips, tensors = mesh.shape["fsdp"] // 2, mesh.shape["tp"]
    in_specs = (P("fsdp", "tp"), P("fsdp", "tp"), P(("tp", "fsdp"), None))
    out_specs = (P("fsdp", "tp"), P("fsdp", "tp"), P(("tp", "fsdp"), None))
    return jax.shard_map(
        functools.partial(shards, chips, tensors),
        mesh=mesh, in_specs=in_specs, out_specs=out_specs, check_vma=False,
    )
```

time: 696 us -> 104 us (0.15)
  waiting for transfers between devices: 530 us -> 0 us
  Pallas kernels: 0 us -> 104 us
  blocking collectives: 73.7 us -> 0 us
  other arithmetic: 56.7 us -> 0 us
  between operations: 15.2 us -> 0.64 us
  matrix products: 10.9 us -> 0 us
    psum x3 -> x0, waiting for transfers between devices: 530 us -> none  [the longest x1 213 us: shards(): projected = lax.psum(partial_proj, 'fsdp')]
    pallas_call x0 -> x2, Pallas kernels: none -> 104 us  [the longest x1 99.7 us: shards(): pl.pallas_call(functools.partial(main_kernel, chips, tensors), out_shape=...]
    another operation x9 -> x0, other arithmetic: 53.7 us -> none  [the longest x6 34 us: orthonormal(): lower = jnp.linalg.cholesky(gram_matrix)]
    all_gather x1 -> x0, blocking collectives: 40.3 us -> none  [shards(): lax.all_gather(right_factor, 'fsdp', axis=0, tiled=True)]
    psum x1 -> x0, blocking collectives: 33.3 us -> none  [shards(): col_sums = lax.psum(jnp.sum(projected * projected, axis=0), 'tp')]
    dot_general x5 -> x0, matrix products: 9.46 us -> none  [the longest x1 2.57 us: shards(): jnp.dot(blend_b, lax.all_gather(right_factor, 'fsdp', axis=0, tiled=True)...]
  transfers between devices with their start and end apart: 3 -> 0, of which waited for: 3 -> 0; matrix products, arithmetic and copies ran while one was open for 0% -> 0% of each run, Pallas kernels for 0% -> 0%
where the time goes in v1:
time: 104 us
  Pallas kernels  104 us (100%)
    pallas_call x1, Pallas kernels, shards(): pl.pallas_call(functools.partial(main_kernel, chips, tensors), out_shape=...  99.7 us
    pallas_call x1, Pallas kernels, shards(): pl.pallas_call(output_kernel, out_shape=[jax.ShapeDtypeStruct((rows, widt...  3.91 us

profile of v1, /device:TPU:1, one launch (start us, length us, event | category | flops | bytes accessed | tf_op | source)
XLA Modules:
  0.0 104.3 jit_solution(13315590380574268331)
XLA Ops:
  0.6 99.7 %main.1 = (bf16[256,256]{1,0:T(8,128)(2,1)}, bf16[1792,256]{1,0:T(8,128)(2,1)}, f32[56,256]{1,0:T(8,128)}, f32[8,256]{1,0:T(8,128)}) custom-call(bf16[256,1792]{1,0:T(8,128)(2,1)} %g_ref.3, bf16[256,1792]{1,0:T(8,128)(2,1)} %m_ref.3, bf16[56,256]{1,0:T(8,128)(2,1)} %r_ref.1), custom_call_target="tpu_custom_call" | custom-call | tf_op jit(solution)/shard_map/main/pallas_call | solution.py:576
  100.4 3.9 %output.1 = (bf16[256,1792]{1,0:T(8,128)(2,1)}, bf16[256,1792]{1,0:T(8,128)(2,1)}, bf16[56,256]{1,0:T(8,128)(2,1)}) custom-call(bf16[256,1792]{1,0:T(8,128)(2,1)} %g_ref.3, bf16[256,1792]{1,0:T(8,128)(2,1)} %m_ref.3, bf16[256,256]{1,0:T(8,128)(2,1)} %get-tuple-element.7.o_ref, bf16[1792,256]{1,0:T(8,128)(2,1)} %get-tuple-element.8.p_ref, ...), custom_call_target="tpu_custom_call" | custom-call | tf_op jit(solution)/shard_map/output/pallas_call | solution.py:629

commit v2 on v1

--- a/solution.py
+++ b/solution.py
@@ -20,7 +20,7 @@
 MESH = pl.DeviceIdType.MESH
 HIGHEST = lax.Precision.HIGHEST
 LANES = 128
-PIVOTS = 32
+PIVOTS = 64
 NEAR = (1, -1, 2, -2)
 FAR = (5, -5)
 RELAY_AT = 64
@@ -151,9 +151,8 @@
 
 
 class Sum:
-    def __init__(self, place, prepare, terms, relays, direct, sums, send_sem, recv_sem):
+    def __init__(self, place, terms, relays, direct, sums, send_sem, recv_sem):
         self.place, self.terms = place, terms
-        self.prepare = prepare
         self.relays, self.direct, self.sums = relays, direct, sums
         self.send_sem, self.recv_sem = send_sem, recv_sem
         self.started = {}
@@ -168,16 +167,10 @@
         place = self.place
         for i, far in enumerate(FAR):
             for j, near in enumerate(NEAR):
-                self.prepare(place.chip(near + far))
                 self.send(4 * i + j, self.terms.at[place.chip(near + far)], self.relays.at[4 * i + j], near)
-        self.prepare(place.chip(8))
         self.send(14, self.terms.at[place.chip(8)], self.relays.at[8], 3 - 6 * place.c)
         for j, near in enumerate(NEAR):
-            self.prepare(place.chip(near))
             self.send(8 + j, self.terms.at[place.chip(near)], self.direct.at[j], near)
-        for far in FAR:
-            self.prepare(place.chip(far))
-        self.prepare(place.z)
 
     def relay(self):
         for i, far in enumerate(FAR):
@@ -310,7 +303,7 @@
     g_here, m_here, r_here, blend_b, slots, right_all, partial, parts, basis, gram, other, pieces, gathered,
     left, right, scale, product, from_partner, terms, relays, direct, relay_sums, projected_slots,
     squares, other_squares, square_parts, square_rows, ortho, projected, own_rows, norm,
-    load_sem, sems_r, recv_r, send_q, recv_q, send_h, recv_h, sems_p, recv_p, send_t, recv_t, send_z, recv_z, send_o, recv_o, store_sem,
+    load_sem, sems_r, recv_r, send_q, recv_q, sems_p, recv_p, send_t, recv_t, send_z, recv_z, send_o, recv_o, store_sem,
 ):
     place = Place(chips, tensors)
     rows, width = g_ref.shape
@@ -400,51 +393,40 @@
 
     gram_swap = swap(0, piece_of(1 - place.c), other)
 
-    splits = []
-    for _ in range(3):
-        splits.append(value.astype(BF16))
-        value = value - splits[-1].astype(F32)
-    basis_b = jnp.concatenate(splits, axis=1)
-    for j in range(0, width, tile):
-        part = lax.dot_general(blend_b[:, j : j + tile], basis_b, contract_rows, preferred_element_type=F32)
-        part = part[:, :rank] + part[:, rank : 2 * rank] + part[:, 2 * rank :]
-        at = j
-        while at < j + tile:
-            chunk, skip = divmod(at, block)
-            most = min(block - skip, j + tile - at)
-            product[chunk // 2, chunk % 2, skip : skip + most, :] = part[at - j : at - j + most]
-            at += most
-    order = [place.chip(near + far) for far in FAR for near in NEAR] + [place.chip(8)]
-    order += [place.chip(steps) for steps in NEAR + FAR] + [place.z]
-    halves = []
-    for i, chip in enumerate(order):
-        half = remote(
-            product.at[chip, 1 - place.c], from_partner.at[chip], send_h.at[0], recv_h.at[i], place.partner()
-        )
-        half.start()
-        halves.append(half)
-
     gram_swap.wait_recv()
     pieces[place.z] = piece_of(place.c)[...] + other[...]
     with jax.named_scope("sum_gram"):
         gram_work = exchange(
             True, 0, lambda z: pieces.at[place.z], pieces.at[place.z], pieces.at[: chips - 1]
         )
-        waiting = list(halves)
-
-        def add_cores(chip):
-            waiting.pop(0).wait_recv()
-            terms[chip] = product[chip, place.c] + from_partner[chip]
-
-        chip_sum = Sum(place, add_cores, terms, relays, direct, relay_sums, send_q.at[0], recv_q)
-        chip_sum.begin()
+        splits = []
+        for _ in range(3):
+            splits.append(value.astype(BF16))
+            value = value - splits[-1].astype(F32)
+        basis_b = jnp.concatenate(splits, axis=1)
+        for j in range(0, width, tile):
+            part = lax.dot_general(blend_b[:, j : j + tile], basis_b, contract_rows, preferred_element_type=F32)
+            part = part[:, :rank] + part[:, rank : 2 * rank] + part[:, 2 * rank :]
+            at = j
+            while at < j + tile:
+                chunk, skip = divmod(at, block)
+                most = min(block - skip, j + tile - at)
+                product[chunk // 2, chunk % 2, skip : skip + most, :] = part[at - j : at - j + most]
+                at += most
+        product_swap = swap(2, product.at[:, 1 - place.c], from_partner)
         for drain in drains:
             drain()
         drains.clear()
+        product_swap.wait_recv()
+
+        def add_cores(k, _):
+            terms[k] = product[k, place.c] + from_partner[k]
+            return 0
+
+        lax.fori_loop(0, chips, add_cores, 0)
+        chip_sum = Sum(place, terms, relays, direct, relay_sums, send_q.at[0], recv_q)
+        chip_sum.begin()
         drains.append(chip_sum.drain)
-        drains.append(
-            remote(from_partner, from_partner, send_h.at[0], recv_h.at[0], place.partner()).wait_send
-        )
         gram_work.wait_recv()
         gathered[place.c, place.t] = total(pieces, chips)
         own = gathered.at[place.c, place.t]
@@ -615,7 +597,7 @@
             pltpu.VMEM((width, rank), BF16),
             pltpu.VMEM((block, rank), F32),
             pltpu.VMEM((8, rank), F32),
-            dma(3), dma(3), dma(chips - 1), dma(1), dma(chips - 1), dma(1), dma(chips), dma(3), dma(chips - 1),
+            dma(3), dma(3), dma(chips - 1), dma(1), dma(chips - 1), dma(3), dma(chips - 1),
             dma(4), dma(4), dma(2), dma(2), dma(4), dma(4), dma(7),
         ],
         compiler_params=pltpu.CompilerParams(

time: 104 us -> 103 us (level); the launches traced: 104 us -> 102 us
  Pallas kernels: 104 us -> 101 us
    pallas_call x1, Pallas kernels: 99.7 us -> 97.4 us  [shards(): pl.pallas_call(functools.partial(main_kernel, chips, tensors), out_shape=...]
where the time goes in v2:
time: 103 us; the launch traced here: 102 us
  Pallas kernels  101 us (98%)
    pallas_call x1, Pallas kernels, shards(): pl.pallas_call(functools.partial(main_kernel, chips, tensors), out_shape=...  97.4 us
    pallas_call x1, Pallas kernels, shards(): pl.pallas_call(output_kernel, out_shape=[jax.ShapeDtypeStruct((rows, widt...  3.92 us

profile of v2, /device:TPU:1, one launch (start us, length us, event | category | flops | bytes accessed | tf_op | source)
XLA Modules:
  0.0 101.9 jit_solution(7443056440848113362)
XLA Ops:
  0.6 97.4 %main.1 = (bf16[256,256]{1,0:T(8,128)(2,1)}, bf16[1792,256]{1,0:T(8,128)(2,1)}, f32[56,256]{1,0:T(8,128)}, f32[8,256]{1,0:T(8,128)}) custom-call(bf16[256,1792]{1,0:T(8,128)(2,1)} %g_ref.3, bf16[256,1792]{1,0:T(8,128)(2,1)} %m_ref.3, bf16[56,256]{1,0:T(8,128)(2,1)} %r_ref.1), custom_call_target="tpu_custom_call" | custom-call | tf_op jit(solution)/shard_map/main/pallas_call | solution.py:558
  98.0 3.9 %output.1 = (bf16[256,1792]{1,0:T(8,128)(2,1)}, bf16[256,1792]{1,0:T(8,128)(2,1)}, bf16[56,256]{1,0:T(8,128)(2,1)}) custom-call(bf16[256,1792]{1,0:T(8,128)(2,1)} %g_ref.3, bf16[256,1792]{1,0:T(8,128)(2,1)} %m_ref.3, bf16[256,256]{1,0:T(8,128)(2,1)} %get-tuple-element.7.o_ref, bf16[1792,256]{1,0:T(8,128)(2,1)} %get-tuple-element.8.p_ref, ...), custom_call_target="tpu_custom_call" | custom-call | tf_op jit(solution)/shard_map/output/pallas_call | solution.py:611
